TPU v7x, 128 devices: a whole 4x4x4 slice. The times are simulated.
128 devices in a mesh: dp: 8 (over x, core), expert: 16 (over z, y).
Axes of the slice: x: 4, y: 4, z: 4, core: 2. Of those that a mesh axis runs over, the one named last changes fastest.
Arguments:
- tokens: bfloat16 [16384, 4096], P(('dp', 'expert')), may hold values from -6 to 6
- norm_gain: float32 [4096], replicated, may hold values from 0.1 to 1.9
- routes: int32 [16384, 1], P(('dp', 'expert')), may hold values from 0 to 7; in each aligned block of 128 rows (0 to 127, 128 to 255, ...) at most 16 rows name the same one
- route_weight: float32 [16384, 1], P(('dp', 'expert')), may hold values from 0.2 to 1
- gate_weight: bfloat16 [8, 1536, 4096], P('dp', 'expert'), may hold values from -0.09375 to 0.09375
- up_weight: bfloat16 [8, 1536, 4096], P('dp', 'expert'), may hold values from -0.09375 to 0.09375
- down_weight: bfloat16 [8, 1536, 4096], P('dp', 'expert'), may hold values from -0.15625 to 0.15625
- cotangent: bfloat16 [16384, 4096], P(('dp', 'expert')), may hold values from -6 to 6
Outputs:
- grad_tokens: bfloat16 [16384, 4096], P(('dp', 'expert'))
- grad_gate: bfloat16 [8, 1536, 4096], P('dp', 'expert')
- grad_up: bfloat16 [8, 1536, 4096], P('dp', 'expert')
- grad_down: bfloat16 [8, 1536, 4096], P('dp', 'expert')
Inputs may be any that keep to these rules, and one draw needn't show every extreme that they name: `routes`: among the tokens of one device exactly 16 have each expert.
All inputs are finite; a program needn't handle non-finite values.
Results may differ from a plain program's by a relative error of at most 0.013.
Values may be sent and summed in bfloat16 or wider, within the bound.
A program may use at most 192 MiB of HBM per device.

v0:
```python
import jax
import jax.numpy as jnp
from jax import lax
from jax.sharding import PartitionSpec as P


def place_matrix(routes, experts, capacity):
    chosen = routes[:, 0]
    onehot = (chosen[:, None] == jnp.arange(experts, dtype=jnp.int32)[None, :]).astype(jnp.int32)
    earlier = jnp.cumsum(onehot, axis=0) - onehot
    position = jnp.sum(earlier * onehot, axis=1)
    slot_ids = chosen * capacity + position
    return (jnp.arange(experts * capacity, dtype=jnp.int32)[:, None] == slot_ids[None, :]).astype(
        jnp.bfloat16
    )


def to_owners(slots):
    arrived = lax.all_to_all(slots, "dp", split_axis=0, concat_axis=0, tiled=True)
    gathered = lax.all_gather(arrived, "expert", axis=0, tiled=True)
    return gathered.reshape(-1, slots.shape[2])


def to_sources(partial_value, groups, experts, capacity):
    model_width = partial_value.shape[1]
    summed = lax.psum_scatter(
        partial_value.astype(jnp.float32)
        .reshape(groups, experts * capacity, model_width)
        .astype(jnp.bfloat16),
        "expert",
        scatter_dimension=0,
        tiled=True,
    )
    local_rows = summed.reshape(experts, capacity, model_width)
    returned = lax.all_to_all(local_rows, "dp", split_axis=0, concat_axis=0, tiled=True)
    return returned.reshape(experts * capacity, model_width)


def contract_first(left, right):
    return lax.dot_general(
        left, right, (((0,), (0,)), ((), ())), preferred_element_type=jnp.float32
    )


def contract_last(left, right):
    return lax.dot_general(
        left, right, (((1,), (1,)), ((), ())), preferred_element_type=jnp.float32
    )


def on_device(
    tokens, norm_gain, routes, route_weight, gate_weight, up_weight, down_weight, cotangent
):
    row_count = tokens.shape[0]
    model_width = tokens.shape[1]
    experts = lax.axis_size("dp")
    groups = lax.axis_size("expert")
    capacity = row_count // experts
    placing = place_matrix(routes, experts, capacity)
    tokens_float = tokens.astype(jnp.float32)
    inv_rms = lax.rsqrt(jnp.mean(tokens_float * tokens_float, axis=-1, keepdims=True) + 1e-06)
    unit_rows = tokens_float * inv_rms
    normed = (unit_rows * norm_gain).astype(jnp.bfloat16)
    send_rows = jnp.dot(placing, normed, preferred_element_type=jnp.float32).astype(jnp.bfloat16)
    row_grad = (route_weight * cotangent.astype(jnp.float32)).astype(jnp.bfloat16)
    grad_slots = jnp.dot(placing, row_grad, preferred_element_type=jnp.float32).astype(jnp.bfloat16)
    send_shaped = send_rows.reshape(experts, capacity, model_width)
    grad_shaped = grad_slots.reshape(experts, capacity, model_width)
    owner_rows = to_owners(send_shaped)
    owner_grads = to_owners(grad_shaped)
    gate_mat = gate_weight[0]
    up_mat = up_weight[0]
    down_mat = down_weight[0]
    gate_pre = contract_last(gate_mat, owner_rows)
    up_pre = contract_last(up_mat, owner_rows)
    sigmoid_gate = jax.nn.sigmoid(gate_pre)
    active = gate_pre * sigmoid_gate
    hidden = (active * up_pre).astype(jnp.bfloat16)
    hidden_grad = contract_last(down_mat, owner_grads)
    gate_act = (
        hidden_grad * up_pre * sigmoid_gate * (1.0 + gate_pre * (1.0 - sigmoid_gate))
    ).astype(jnp.bfloat16)
    up_act = (hidden_grad * active).astype(jnp.bfloat16)
    grad_gate = jnp.dot(gate_act, owner_rows, preferred_element_type=jnp.float32).astype(
        jnp.bfloat16
    )
    grad_up = jnp.dot(up_act, owner_rows, preferred_element_type=jnp.float32).astype(jnp.bfloat16)
    grad_down = jnp.dot(hidden, owner_grads, preferred_element_type=jnp.float32).astype(
        jnp.bfloat16
    )
    partial_in = (contract_first(gate_act, gate_mat) + contract_first(up_act, up_mat)).astype(
        jnp.bfloat16
    )
    normed_grad = to_sources(partial_in, groups, experts, capacity)
    scaled_grad = contract_first(placing, normed_grad) * norm_gain
    moved_grad = inv_rms * (
        scaled_grad - unit_rows * jnp.mean(scaled_grad * unit_rows, axis=-1, keepdims=True)
    )
    grad_tokens = (cotangent.astype(jnp.float32) + moved_grad).astype(jnp.bfloat16)
    return (grad_tokens, grad_gate[None], grad_up[None], grad_down[None])


def solution(mesh):
    placed = (
        P(("dp", "expert"), None),
        P(),
        P(("dp", "expert"), None),
        P(("dp", "expert"), None),
        P("dp", "expert", None),
        P("dp", "expert", None),
        P("dp", "expert", None),
        P(("dp", "expert"), None),
    )
    return jax.shard_map(
        on_device,
        mesh=mesh,
        in_specs=placed,
        out_specs=(
            P(("dp", "expert"), None),
            P("dp", "expert", None),
            P("dp", "expert", None),
            P("dp", "expert", None),
        ),
        check_vma=False,
    )
```

profile of v0, /device:TPU:1, one launch (start us, length us, event | category | flops | bytes accessed | tf_op | source)
XLA Modules:
  0.0 441.1 jit_solution(12762106594437603405)
XLA Ops:
  7.2 0.0 all-gather.5.cloned.1.call-start
  7.2 1.6 fusion.12
  8.8 0.7 fusion.26
  9.6 0.2 reduce_window_sum.11
  9.7 0.8 select_reduce_fusion
  10.6 0.7 multiply_add_fusion
  11.2 1.7 convolution_convert_fusion
  13.0 20.9 %all_to_all.15 = bf16[8,16,4096]{2,1,0:T(8,128)(2,1)} all-to-all(bf16[8,16,4096]{2,1,0:T(8,128)(2,1)S(1)} %bitcast.57), channel_id=1, replica_groups=mesh['dp'=8,'expert'=16] {'dp'}, dimensions={0} | all-to-all | bytes 2097152 | tf_op jit(solution)/shard_map/all_to_all | solution.py:19
  33.9 0.0 all-gather.5.cloned.1.call-update
  33.9 0.0 all-gather.3.cloned.1.call-start
  34.0 0.5 convolution_convert_fusion.1
  34.5 19.2 %all_to_all.16 = bf16[8,16,4096]{2,1,0:T(8,128)(2,1)} all-to-all(bf16[8,16,4096]{2,1,0:T(8,128)(2,1)S(1)} %bitcast.58), channel_id=1, replica_groups=mesh['dp'=8,'expert'=16] {'dp'}, dimensions={0} | all-to-all | bytes 2097152 | tf_op jit(solution)/shard_map/all_to_all | solution.py:19
  53.7 0.0 all-gather.3.cloned.1.call-update
  53.8 0.0 reduce-scatter.4.cloned.1.call-start
  53.8 92.6 %all-gather.5.cloned.1.call-done = bf16[128,16,4096]{2,1,0:T(8,128)(2,1)} async-done(((bf16[8,16,4096]{2,1,0:T(8,128)(2,1)}), bf16[128,16,4096]{2,1,0:T(8,128)(2,1)}) %all-gather.5.cloned.1.call-update) | async-done | bytes 16777232 | tf_op jit(solution)/shard_map/all_gather | solution.py:20
  146.4 11.2 %convolution_bitcast_fusion = f32[96,2048]{1,0:T(8,128)S(1)} fusion(bf16[2048,4096]{1,0:T(8,128)(2,1)} %bitcast.49, bf16[1,96,4096]{2,1,0:T(8,128)(2,1)S(1)} %copy-done), kind=kOutput, calls=%fused_computation.17 | convolution fusion | flops 1610612736 | bytes 18350080 | tf_op jit(solution)/shard_map/dot_general | solution.py:46
  157.6 5.2 %convolution_bitcast_fusion.1 = f32[96,2048]{1,0:T(8,128)S(1)} fusion(bf16[2048,4096]{1,0:T(8,128)(2,1)S(1)} %bitcast.52, bf16[1,96,4096]{2,1,0:T(8,128)(2,1)S(1)} %copy-done.6), kind=kOutput, calls=%fused_computation.18 | convolution fusion | flops 1610612736 | bytes 18350080 | tf_op jit(solution)/shard_map/dot_general | solution.py:46
  162.9 96.8 %all-gather.3.cloned.1.call-done = bf16[128,16,4096]{2,1,0:T(8,128)(2,1)} async-done(((bf16[8,16,4096]{2,1,0:T(8,128)(2,1)}), bf16[128,16,4096]{2,1,0:T(8,128)(2,1)}) %all-gather.3.cloned.1.call-update) | async-done | bytes 16777232 | tf_op jit(solution)/shard_map/all_gather | solution.py:20
  259.6 11.2 %multiply_convert_fusion.1 = (bf16[96,2048]{1,0:T(8,128)(2,1)S(1)}, bf16[96,2048]{1,0:T(8,128)(2,1)S(1)}) fusion(f32[96,2048]{1,0:T(8,128)S(1)} %convolution_bitcast_fusion, f32[96,2048]{1,0:T(8,128)S(1)} %convolution_bitcast_fusion.1, bf16[2048,4096]{1,0:T(8,128)(2,1)} %bitcast.54, bf16[1,96,4096]{2,1,0:T(8,128)(2,1)} %param.14), kind=kOutput, calls=%fused_computation.37 | convolution fusion | flops 1613168640 | bytes 19922944 | tf_op jit(solution)/shard_map/dot_general | solution.py:46
  270.9 13.3 %fusion.18 = f32[2048,4096]{1,0:T(8,128)} fusion(bf16[96,2048]{1,0:T(8,128)(2,1)S(1)} %get-tuple-element.5, bf16[1,96,4096]{2,1,0:T(8,128)(2,1)S(1)} %copy-done), kind=kOutput, calls=%fused_computation.30 | convolution fusion | flops 1610612736 | bytes 34734080 | tf_op jit(solution)/shard_map/dot_general | solution.py:40
  284.2 17.0 %add_convert_fusion = bf16[2048,4096]{1,0:T(8,128)(2,1)} fusion(f32[2048,4096]{1,0:T(8,128)} %fusion.18, bf16[96,2048]{1,0:T(8,128)(2,1)S(1)} %get-tuple-element.4, bf16[1,96,4096]{2,1,0:T(8,128)(2,1)S(1)} %copy-done.6), kind=kOutput, calls=%fused_computation | convolution fusion | flops 1627389952 | bytes 51511296 | tf_op jit(solution)/shard_map/dot_general | solution.py:40
  301.1 0.0 reduce-scatter.4.cloned.1.call-update
  301.2 1.0 copy-done.8
  302.1 9.4 %fusion.1 = bf16[1,96,4096]{2,1,0:T(8,128)(2,1)} fusion(bf16[96,2048]{1,0:T(8,128)(2,1)S(1)} %copy-done.8, bf16[2048,4096]{1,0:T(8,128)(2,1)} %bitcast.50), kind=kOutput, calls=%fused_computation.8 | convolution fusion | flops 1611005952 | bytes 17956864 | tf_op jit(solution)/shard_map/dot_general | solution.py:87
  311.5 9.5 %fusion.2 = bf16[1,96,4096]{2,1,0:T(8,128)(2,1)} fusion(bf16[2048,4096]{1,0:T(8,128)(2,1)} %bitcast.55, f32[96,2048]{1,0:T(8,128)S(1)} %convolution_bitcast_fusion.1, f32[96,2048]{1,0:T(8,128)S(1)} %convolution_bitcast_fusion), kind=kOutput, calls=%fused_computation.9 | convolution fusion | flops 1612185600 | bytes 19136512 | tf_op jit(solution)/shard_map/dot_general | solution.py:88
  321.0 90.3 %reduce-scatter.4.cloned.1.call-done = bf16[1,128,4096]{2,1,0:T(8,128)(2,1)} async-done(((bf16[16,128,4096]{2,1,0:T(8,128)(2,1)}), bf16[1,128,4096]{2,1,0:T(8,128)(2,1)}) %reduce-scatter.4.cloned.1.call-update) | async-done | bytes 1048592
  411.4 5.2 %all-to-all-start.2 = ((bf16[8,16,4096]{2,1,0:T(8,128)(2,1)}), bf16[8,16,4096]{2,1,0:T(8,128)(2,1)S(1)}, u32[]{:S(2)}, u32[]{:S(2)}) async-start(bf16[8,16,4096]{2,1,0:T(8,128)(2,1)} %bitcast.59), calls=%async_computation.2 | async-start | bytes 2097152 | tf_op jit(solution)/shard_map/all_to_all | solution.py:35
  416.6 9.5 %fusion = bf16[1,96,4096]{2,1,0:T(8,128)(2,1)} fusion(bf16[96,2048]{1,0:T(8,128)(2,1)S(1)} %get-tuple-element.5, bf16[2048,4096]{1,0:T(8,128)(2,1)} %bitcast.51), kind=kOutput, calls=%fused_computation.7 | convolution fusion | flops 1611005952 | bytes 17956864 | tf_op jit(solution)/shard_map/dot_general | solution.py:84
  426.1 5.6 %all-to-all-done.2 = bf16[8,16,4096]{2,1,0:T(8,128)(2,1)S(1)} async-done(((bf16[8,16,4096]{2,1,0:T(8,128)(2,1)}), bf16[8,16,4096]{2,1,0:T(8,128)(2,1)S(1)}, u32[]{:S(2)}, u32[]{:S(2)}) %all-to-all-start.2) | async-done | bytes 1048608 | tf_op jit(solution)/shard_map/all_to_all | solution.py:35
  431.7 0.7 fusion.9
  432.4 0.5 copy-done.5
  432.9 1.6 fusion.7
  (22 shorter events, 0.1 us)
Async XLA Ops:
  7.2 139.2 %copy-start = (bf16[1,96,4096]{2,1,0:T(8,128)(2,1)S(1)}, bf16[1,96,4096]{2,1,0:T(8,128)(2,1)}, u32[]{:S(2)}) copy-start(bf16[1,96,4096]{2,1,0:T(8,128)(2,1)} %param.12) | copy-start | bytes 2359300
  7.2 139.2 %all-gather.5.cloned.1.call-start = ((), (), s32[]{:S(2)}) async-start(), calls=%async_computation.5 | async-start | bytes 17825792 | tf_op jit(solution)/shard_map/all_gather | solution.py:20
  13.0 21.0 %copy-start.4 = (bf16[128,4096]{1,0:T(8,128)(2,1)S(1)}, bf16[128,4096]{1,0:T(8,128)(2,1)}, u32[]{:S(2)}) copy-start(bf16[128,4096]{1,0:T(8,128)(2,1)} %param.15) | copy-start | bytes 3145732
  13.0 21.0 %copy-start.10 = (f32[128,1]{0,1:T(1,128)S(1)}, f32[128,1]{0,1:T(1,128)}, u32[]{:S(2)}) copy-start(f32[128,1]{0,1:T(1,128)} %param.11) | copy-start | bytes 1540
  33.9 225.7 %all-gather.3.cloned.1.call-start = ((), (), s32[]{:S(2)}) async-start(), calls=%async_computation.4 | async-start | bytes 17825792 | tf_op jit(solution)/shard_map/all_gather | solution.py:20
  53.8 357.6 %reduce-scatter.4.cloned.1.call-start = ((), (), s32[]{:S(2)}) async-start(), calls=%async_computation.6 | async-start | bytes 17825792
  146.4 11.2 %copy-start.2 = (bf16[128,16,4096]{2,1,0:T(8,128)(2,1)S(1)}, bf16[128,16,4096]{2,1,0:T(8,128)(2,1)}, u32[]{:S(2)}) copy-start(bf16[128,16,4096]{2,1,0:T(8,128)(2,1)} %all-gather.5.cloned.1.call-done) | copy-start | bytes 50331652
  146.4 11.2 %copy-start.6 = (bf16[1,96,4096]{2,1,0:T(8,128)(2,1)S(1)}, bf16[1,96,4096]{2,1,0:T(8,128)(2,1)}, u32[]{:S(2)}) copy-start(bf16[1,96,4096]{2,1,0:T(8,128)(2,1)} %param.13) | copy-start | bytes 2359300
  270.9 13.3 %copy-start.7 = (bf16[96,2048]{1,0:T(8,128)(2,1)}, bf16[96,2048]{1,0:T(8,128)(2,1)S(1)}, u32[]{:S(2)}) copy-start(bf16[96,2048]{1,0:T(8,128)(2,1)S(1)} %get-tuple-element.4) | copy-start | bytes 1179652
  301.1 1.0 copy-start.8
  411.4 20.3 %all-to-all-start.2 = ((bf16[8,16,4096]{2,1,0:T(8,128)(2,1)}), bf16[8,16,4096]{2,1,0:T(8,128)(2,1)S(1)}, u32[]{:S(2)}, u32[]{:S(2)}) async-start(bf16[8,16,4096]{2,1,0:T(8,128)(2,1)} %bitcast.59), calls=%async_computation.2 | async-start | bytes 2097152 | tf_op jit(solution)/shard_map/all_to_all | solution.py:35
  416.6 15.1 %copy-start.3 = (bf16[128,4096]{1,0:T(8,128)(2,1)S(1)}, bf16[128,4096]{1,0:T(8,128)(2,1)}, u32[]{:S(2)}) copy-start(bf16[128,4096]{1,0:T(8,128)(2,1)} %param.8) | copy-start | bytes 3145732
  416.6 15.1 %copy-start.9 = (f32[4096]{0:T(1024)S(1)}, f32[4096]{0:T(1024)}, u32[]{:S(2)}) copy-start(f32[4096]{0:T(1024)} %param.9) | copy-start | bytes 49156
  431.7 1.2 copy-start.5
  432.4 2.2 copy-start.1
Sparse Core Ops, SparseCore 0:
  34.1 112.3 all-gather.4
  148.5 111.0 all-gather.2
  301.3 110.0 reduce-scatter.3
where the time goes:
time: 442 us; the launch traced here: 441 us
  waiting for transfers between devices  285 us (64%)
  matrix products  89.2 us (20%)
  blocking collectives  40.1 us (9%)
  between operations  13.9 us (3%)
  other arithmetic  5.63 us (1%)
  starting transfers between devices  5.34 us (1%)
    all_gather x2, waiting for transfers between devices, to_owners(): gathered = lax.all_gather(arrived, 'expert', axis=0, tiled=True)  189 us
    unnamed x4, waiting for transfers between devices  90.4 us
    all_to_all x2, blocking collectives, to_owners(): lax.all_to_all(slots, 'dp', split_axis=0, concat_axis=0, tiled=True)  40.1 us
    dot_general x3, matrix products, contract_first(): lax.dot_general(left, right, (((0,), (0,)), ((), ())), preferred_element_...  30.9 us
    dot_general x3, matrix products, contract_last(): lax.dot_general(left, right, (((1,), (1,)), ((), ())), preferred_element_...  27.6 us
    dot_general x1, matrix products, on_device(): jnp.dot(gate_act, owner_rows, preferred_element_type=jnp.float32)  9.5 us
    dot_general x1, matrix products, on_device(): jnp.dot(hidden, owner_grads, preferred_element_type=jnp.float32)  9.5 us
    dot_general x1, matrix products, on_device(): jnp.dot(up_act, owner_rows, preferred_element_type=jnp.float32)  9.42 us
  transfers between devices with their start and end apart: 4, of which 4 were waited for; matrix products, arithmetic and copies ran while one was open for 10% of the time, Pallas kernels for 0%

commit v1 on v0

v1 whole, which is shorter than its diff:
```python
import functools

import jax
import jax.numpy as jnp
from jax import lax
from jax.experimental import pallas as pl
from jax.experimental.pallas import tpu as pltpu
from jax.sharding import PartitionSpec as P

MESH = pl.DeviceIdType.MESH
F32, BF16 = jnp.float32, jnp.bfloat16
D = 4096
TOK = 128
CAP = 16
HID = 96
HALF = 64
COLS = 512
SLOTS = 4

N_REMOTE = 80
N_LOCAL = 16


def dot(left, right, left_dim, right_dim):
    return lax.dot_general(
        left, right, (((left_dim,), (right_dim,)), ((), ())), preferred_element_type=F32
    )


def kernel(
    tok_hbm, cot_hbm, gain_ref, routes_ref, rw_ref, gate_hbm, up_hbm, down_hbm,
    gt_hbm, gg_hbm, gu_hbm, gd_hbm,
    tok, cot, norm, rgrad, send_n, send_g, place, inv,
    rn, rg, wgu, wd, pre, hg, act, act_t, hid,
    part, ptl, ptr, pfl, pfr, ret_send, ret, qbuf, out_t,
    pg, pd, gtl, gtr, gfl, gfr,
    ssem, rsem, lsem,
):
    dp = lax.axis_index("dp")
    ex = lax.axis_index("expert")
    core = lax.rem(dp, 2)
    rstride = 1 + 3 * core
    wstride = 4 - 3 * core
    rpos = lax.rem(lax.div(ex, rstride), 4)
    wpos = lax.rem(lax.div(ex, wstride), 4)
    r_right = (dp, ex + rstride * (lax.rem(rpos + 1, 4) - rpos))
    r_left = (dp, ex + rstride * (lax.rem(rpos + 3, 4) - rpos))
    w_right = (dp, ex + wstride * (lax.rem(wpos + 1, 4) - wpos))
    w_left = (dp, ex + wstride * (lax.rem(wpos + 3, 4) - wpos))

    count = [0, 0]
    sent = []

    def local(src, dst):
        copy = pltpu.make_async_copy(src, dst, lsem.at[count[1]])
        count[1] += 1
        copy.start()
        return copy

    def remote(src, dst, device):
        copy = pltpu.make_async_remote_copy(
            src_ref=src, dst_ref=dst, send_sem=ssem.at[count[0]], recv_sem=rsem.at[count[0]],
            device_id=device, device_id_type=MESH,
        )
        count[0] += 1
        copy.start()
        sent.append(copy)
        return copy

    tok_in = local(tok_hbm, tok)
    cot_in = local(cot_hbm, cot)

    barrier = pltpu.get_barrier_semaphore()
    partners = [r_right, r_left, w_right, w_left]
    partners += [(lax.rem(dp + k, 8), ex) for k in range(1, 8)]
    for device in partners:
        pl.semaphore_signal(barrier, inc=1, device_id=device, device_id_type=MESH)
    pl.semaphore_wait(barrier, len(partners))

    w_from_left, w_from_right = [], []
    places = [(gate_hbm, wgu, 192, 0), (up_hbm, wgu, 192, 96), (down_hbm, wd, 96, 0)]
    for src, buf, step, at in places:
        w_from_left.append(remote(src, buf.at[pl.ds(step + at, HID)], w_right))
        w_from_right.append(remote(src, buf.at[pl.ds(2 * step + at, HID)], w_left))
    w_own = [local(src, buf.at[pl.ds(at, HID)]) for src, buf, step, at in places]

    chosen = routes_ref[...]
    lane = lax.broadcasted_iota(jnp.int32, (TOK, TOK), 1)
    sub = lax.broadcasted_iota(jnp.int32, (TOK, TOK), 0)
    onehot = (chosen == lane).astype(F32)
    earlier = dot((lane < sub).astype(F32).astype(BF16), onehot.astype(BF16), 1, 0)
    position = jnp.sum(earlier * onehot, axis=1, keepdims=True)
    piece = jnp.bitwise_and(dp - chosen + 8, 7)
    slot = piece.astype(F32) * CAP + position
    place[...] = (slot == lane.astype(F32)).astype(F32).astype(BF16)

    tok_in.wait()
    cot_in.wait()

    def norm_rows(i, carry):
        rows = pl.ds(pl.multiple_of(i * 16, 16), 16)
        x = tok[rows, :].astype(F32)
        scale = lax.rsqrt(jnp.mean(x * x, axis=-1, keepdims=True) + 1e-06)
        inv[rows, :] = jnp.broadcast_to(scale, (16, 128))
        norm[rows, :] = ((x * scale) * gain_ref[...]).astype(BF16)
        rgrad[rows, :] = (rw_ref[rows, :] * cot[rows, :].astype(F32)).astype(BF16)
        return carry

    lax.fori_loop(0, TOK // 16, norm_rows, 0)

    placing_t = place[...].astype(F32).T.astype(BF16)

    def place_rows(i, carry):
        cols = pl.ds(pl.multiple_of(i * COLS, COLS), COLS)
        send_n[:, cols] = dot(placing_t, norm[:, cols], 1, 0).astype(BF16)
        send_g[:, cols] = dot(placing_t, rgrad[:, cols], 1, 0).astype(BF16)
        return carry

    lax.fori_loop(0, D // COLS, place_rows, 0)

    def at_piece(k):
        return pl.ds((k // 4) * 256 + (k % 4) * CAP, CAP)

    arrive = {0: [], 1: []}
    rn[at_piece(0), :] = send_n[pl.ds(0, CAP), :]
    rg[at_piece(0), :] = send_g[pl.ds(0, CAP), :]
    for k in range(1, 8):
        owner = (lax.rem(dp + 8 - k, 8), ex)
        piece_rows = pl.ds(k * CAP, CAP)
        arrive[k // 4].append(remote(send_n.at[piece_rows], rn.at[at_piece(k)], owner))
        arrive[k // 4].append(remote(send_g.at[piece_rows], rg.at[at_piece(k)], owner))

    w_from_left[0].wait_recv()
    w_last = [remote(wgu.at[pl.ds(192, HID)], wgu.at[pl.ds(3 * 192, HID)], w_right)]
    w_from_right[0].wait_recv()
    w_from_left[1].wait_recv()
    w_from_right[1].wait_recv()
    w_last.append(remote(wgu.at[pl.ds(2 * 192 + 96, HID)], wgu.at[pl.ds(3 * 192 + 96, HID)], w_left))
    w_from_left[2].wait_recv()
    w_last.append(remote(wd.at[pl.ds(HID, 48)], wd.at[pl.ds(3 * HID, 48)], w_right))
    w_from_right[2].wait_recv()
    w_last.append(remote(wd.at[pl.ds(2 * HID + 48, 48)], wd.at[pl.ds(3 * HID + 48, 48)], w_left))

    def row_slot(half, s, at=0, size=HALF):
        return pl.ds(half * 256 + s * HALF + at, size)

    def send_own(buf, half):
        return (
            remote(buf.at[row_slot(half, 0)], buf.at[row_slot(half, 1)], r_right),
            remote(buf.at[row_slot(half, 0)], buf.at[row_slot(half, 2)], r_left),
        )

    def pass_on(buf, half, first):
        first[0].wait_recv()
        a = remote(buf.at[row_slot(half, 1, 0, 32)], buf.at[row_slot(half, 3, 0, 32)], r_right)
        first[1].wait_recv()
        b = remote(buf.at[row_slot(half, 2, 32, 32)], buf.at[row_slot(half, 3, 32, 32)], r_left)
        return a, b

    for copy in arrive[0]:
        copy.wait_recv()
    own_an = send_own(rn, 0)
    own_ag = send_own(rg, 0)
    for copy in arrive[1]:
        copy.wait_recv()
    own_bn = send_own(rn, 1)
    last_a = [*pass_on(rn, 0, own_an), *pass_on(rg, 0, own_ag)]
    own_bg = send_own(rg, 1)
    last_b = [*pass_on(rn, 1, own_bn), *pass_on(rg, 1, own_bg)]

    for copy in (*w_own,):
        copy.wait()
    for copy in w_last:
        copy.wait_recv()

    def activations(half):
        rows = pl.ds(half * 256, 256)

        def per_slot(s, carry):
            two = pl.ds(pl.multiple_of(s * 192, 96), 192)
            one = pl.ds(pl.multiple_of(s * HID, HID), HID)
            pre[...] = dot(wgu[two, :], rn[rows, :], 1, 1)
            hidden_grad = dot(wd[one, :], rg[rows, :], 1, 1)
            gate = pre[pl.ds(0, HID), :]
            up = pre[pl.ds(HID, HID), :]
            sig = jax.nn.sigmoid(gate)
            active = gate * sig
            hid[one, rows] = (active * up).astype(BF16)
            act[pl.ds(pl.multiple_of(s * 192, 96), HID), rows] = (
                hidden_grad * up * sig * (1.0 + gate * (1.0 - sig))
            ).astype(BF16)
            act[pl.ds(pl.multiple_of(s * 192 + HID, 96), HID), rows] = (hidden_grad * active).astype(BF16)
            return carry

        lax.fori_loop(0, SLOTS, per_slot, 0)

    def partials(half):
        rows = pl.ds(half * 256, 256)
        act_t[...] = act[:, rows].astype(F32).T.astype(BF16)

        def per_cols(i, carry):
            cols = pl.ds(pl.multiple_of(i * COLS, COLS), COLS)
            part[rows, cols] = dot(act_t[...], wgu[:, cols], 1, 0).astype(BF16)
            return carry

        lax.fori_loop(0, D // COLS, per_cols, 0)

    def add_into(buf, start, other, at, size):
        def per_rows(i, carry):
            mine = pl.ds(pl.multiple_of(start + i * 16, 16), 16)
            theirs = pl.ds(pl.multiple_of(at + i * 16, 16), 16)
            buf[mine, :] = (buf[mine, :].astype(F32) + other[theirs, :].astype(F32)).astype(BF16)
            return carry

        lax.fori_loop(0, size // 16, per_rows, 0)

    def scatter_start(half):
        through = [
            remote(part.at[row_slot(half, 3, 0, 32)], ptl.at[pl.ds(half * 32, 32)], r_right),
            remote(part.at[row_slot(half, 3, 32, 32)], ptr.at[pl.ds(half * 32, 32)], r_left),
        ]
        plain = [
            remote(part.at[row_slot(half, 2, 32, 32)], pfl.at[pl.ds(half * 64 + 32, 32)], r_right),
            remote(part.at[row_slot(half, 1, 0, 32)], pfr.at[pl.ds(half * 64, 32)], r_left),
        ]
        return through, plain

    def scatter_add(half, through):
        through[0].wait_recv()
        add_into(part, half * 256 + 2 * HALF, ptl, half * 32, 32)
        a = remote(part.at[row_slot(half, 2, 0, 32)], pfl.at[pl.ds(half * 64, 32)], r_right)
        through[1].wait_recv()
        add_into(part, half * 256 + HALF + 32, ptr, half * 32, 32)
        b = remote(part.at[row_slot(half, 1, 32, 32)], pfr.at[pl.ds(half * 64 + 32, 32)], r_left)
        return a, b

    def scatter_end(half, copies):
        for copy in copies:
            copy.wait_recv()

        def per_rows(i, carry):
            mine = pl.ds(pl.multiple_of(half * 256 + i * 16, 16), 16)
            got = pl.ds(pl.multiple_of(half * 64 + i * 16, 16), 16)
            ret_send[got, :] = (
                part[mine, :].astype(F32) + pfl[got, :].astype(F32) + pfr[got, :].astype(F32)
            ).astype(BF16)
            return carry

        lax.fori_loop(0, HALF // 16, per_rows, 0)
        back = []
        for k in range(half * 4, half * 4 + 4):
            piece_rows = pl.ds(k * CAP, CAP)
            if k == 0:
                ret[piece_rows, :] = ret_send[piece_rows, :]
            else:
                source = (lax.rem(dp + k, 8), ex)
                back.append(remote(ret_send.at[piece_rows], ret.at[piece_rows], source))
        return back

    def weight_grads(s):
        two = pl.ds(s * 192, 192)
        one = pl.ds(s * HID, HID)

        def per_cols(i, carry):
            cols = pl.ds(pl.multiple_of(i * COLS, COLS), COLS)
            pg[two, cols] = dot(act[two, :], rn[:, cols], 1, 0).astype(BF16)
            pd[one, cols] = dot(hid[one, :], rg[:, cols], 1, 0).astype(BF16)
            return carry

        lax.fori_loop(0, D // COLS, per_cols, 0)

    for copy in last_a:
        copy.wait_recv()
    activations(0)
    partials(0)
    through_a, plain_a = scatter_start(0)

    for copy in last_b:
        copy.wait_recv()
    activations(1)
    summed_a = scatter_add(0, through_a)
    partials(1)
    through_b, plain_b = scatter_start(1)
    back = scatter_end(0, [*plain_a, *summed_a])

    weight_grads(3)
    grad_through = [
        remote(pg.at[pl.ds(3 * 192, HID)], gtl.at[pl.ds(0, HID)], w_right),
        remote(pg.at[pl.ds(3 * 192 + HID, HID)], gtr.at[pl.ds(0, HID)], w_left),
        remote(pd.at[pl.ds(3 * HID, 48)], gtl.at[pl.ds(HID, 48)], w_right),
        remote(pd.at[pl.ds(3 * HID + 48, 48)], gtr.at[pl.ds(HID, 48)], w_left),
    ]
    summed_b = scatter_add(1, through_b)
    weight_grads(2)
    grad_plain = [
        remote(pg.at[pl.ds(2 * 192 + HID, HID)], gfl.at[pl.ds(HID, HID)], w_right),
        remote(pd.at[pl.ds(2 * HID + 48, 48)], gfl.at[pl.ds(2 * HID + 48, 48)], w_right),
    ]
    weight_grads(1)
    grad_plain += [
        remote(pg.at[pl.ds(192, HID)], gfr.at[pl.ds(0, HID)], w_left),
        remote(pd.at[pl.ds(HID, 48)], gfr.at[pl.ds(2 * HID, 48)], w_left),
    ]
    back += scatter_end(1, [*plain_b, *summed_b])
    weight_grads(0)

    grad_through[0].wait_recv()
    add_into(pg, 2 * 192, gtl, 0, HID)
    grad_summed = [remote(pg.at[pl.ds(2 * 192, HID)], gfl.at[pl.ds(0, HID)], w_right)]
    grad_through[1].wait_recv()
    add_into(pg, 192 + HID, gtr, 0, HID)
    grad_summed.append(remote(pg.at[pl.ds(192 + HID, HID)], gfr.at[pl.ds(HID, HID)], w_left))
    grad_through[2].wait_recv()
    add_into(pd, 2 * HID, gtl, HID, 48)
    grad_summed.append(remote(pd.at[pl.ds(2 * HID, 48)], gfl.at[pl.ds(2 * HID, 48)], w_right))
    grad_through[3].wait_recv()
    add_into(pd, HID + 48, gtr, HID, 48)
    grad_summed.append(remote(pd.at[pl.ds(HID + 48, 48)], gfr.at[pl.ds(2 * HID + 48, 48)], w_left))

    for copy in back:
        copy.wait_recv()
    scale = inv[:, 0:1]

    def scaled(i, total):
        cols = pl.ds(pl.multiple_of(i * COLS, COLS), COLS)
        q = dot(place[...], ret[:, cols], 1, 0) * gain_ref[:, cols]
        qbuf[:, cols] = q
        return total + jnp.sum(q * (tok[:, cols].astype(F32) * scale), axis=-1, keepdims=True)

    total = lax.fori_loop(0, D // COLS, scaled, jnp.zeros((TOK, 1), F32))
    mean = total * (1.0 / D)

    def moved(i, carry):
        cols = pl.ds(pl.multiple_of(i * COLS, COLS), COLS)
        unit = tok[:, cols].astype(F32) * scale
        out_t[:, cols] = (cot[:, cols].astype(F32) + scale * (qbuf[:, cols] - unit * mean)).astype(BF16)
        return carry

    lax.fori_loop(0, D // COLS, moved, 0)
    outs = [local(out_t, gt_hbm)]

    def grad_end(buf, at, got, copies, dst):
        for copy in copies:
            copy.wait_recv()
        add_three(buf, at, got)
        outs.append(local(buf.at[pl.ds(at, HID)], dst))

    def add_three(buf, at, got):
        def per_rows(i, carry):
            mine = pl.ds(pl.multiple_of(at + i * 16, 16), 16)
            theirs = pl.ds(pl.multiple_of(got + i * 16, 16), 16)
            buf[mine, :] = (
                buf[mine, :].astype(F32) + gfl[theirs, :].astype(F32) + gfr[theirs, :].astype(F32)
            ).astype(BF16)
            return carry

        lax.fori_loop(0, HID // 16, per_rows, 0)

    grad_end(pg, 0, 0, [grad_summed[0], grad_plain[2]], gg_hbm)
    grad_end(pg, HID, HID, [grad_plain[0], grad_summed[1]], gu_hbm)
    grad_end(pd, 0, 2 * HID, [grad_plain[1], grad_plain[3], grad_summed[2], grad_summed[3]], gd_hbm)

    for copy in outs:
        copy.wait()
    for copy in sent:
        copy.wait_send()


def on_device(
    tokens, norm_gain, routes, route_weight, gate_weight, up_weight, down_weight, cotangent
):
    any_spec = pl.BlockSpec(memory_space=pl.ANY)
    vmem_spec = pl.BlockSpec(memory_space=pltpu.VMEM)
    rows = lambda n, t=BF16: pltpu.VMEM((n, D), t)
    outs = pl.pallas_call(
        kernel,
        out_shape=(
            jax.ShapeDtypeStruct((TOK, D), BF16),
            jax.ShapeDtypeStruct((HID, D), BF16),
            jax.ShapeDtypeStruct((HID, D), BF16),
            jax.ShapeDtypeStruct((HID, D), BF16),
        ),
        in_specs=[any_spec, any_spec, vmem_spec, vmem_spec, vmem_spec, any_spec, any_spec, any_spec],
        out_specs=(any_spec,) * 4,
        scratch_shapes=[
            rows(TOK), rows(TOK), rows(TOK), rows(TOK), rows(TOK), rows(TOK),
            pltpu.VMEM((TOK, TOK), BF16), pltpu.VMEM((TOK, 128), F32),
            rows(512), rows(512), rows(768), rows(384),
            pltpu.VMEM((192, 256), F32), pltpu.VMEM((8, 128), F32),
            pltpu.VMEM((768, 512), BF16), pltpu.VMEM((256, 768), BF16), pltpu.VMEM((384, 512), BF16),
            rows(512), rows(64), rows(64), rows(128), rows(128),
            rows(TOK), rows(TOK), rows(TOK, F32), rows(TOK),
            rows(768), rows(384), rows(144), rows(144), rows(288), rows(288),
            pltpu.SemaphoreType.DMA((N_REMOTE,)),
            pltpu.SemaphoreType.DMA((N_REMOTE,)),
            pltpu.SemaphoreType.DMA((N_LOCAL,)),
        ],
        compiler_params=pltpu.CompilerParams(
            collective_id=0, has_side_effects=True, vmem_limit_bytes=63 * 2**20
        ),
        cost_estimate=pl.CostEstimate(flops=13 * 10**9, bytes_accessed=9 * 2**20, transcendentals=2**18),
        name="learner_step",
    )(
        tokens, cotangent, norm_gain.reshape(1, D), routes, route_weight,
        gate_weight[0], up_weight[0], down_weight[0],
    )
    return (outs[0], outs[1][None], outs[2][None], outs[3][None])


def solution(mesh):
    token_spec = P(("dp", "expert"), None)
    weight_spec = P("dp", "expert", None)
    return jax.shard_map(
        on_device,
        mesh=mesh,
        in_specs=(token_spec, P(), token_spec, token_spec, weight_spec, weight_spec, weight_spec, token_spec),
        out_specs=(token_spec, weight_spec, weight_spec, weight_spec),
        check_vma=False,
    )
```

time: 442 us -> 156 us (0.35)
  waiting for transfers between devices: 285 us -> 0 us
  Pallas kernels: 0 us -> 146 us
  matrix products: 89.2 us -> 0 us
  blocking collectives: 40.1 us -> 0 us
  between operations: 13.9 us -> 0.66 us
  local copies, waits for them, and re-layouts: 1.56 us -> 8.21 us
  other arithmetic: 5.63 us -> 0 us
  starting transfers between devices: 5.34 us -> 0 us
    all_gather x2 -> x0, waiting for transfers between devices: 189 us -> none  [to_owners(): gathered = lax.all_gather(arrived, 'expert', axis=0, tiled=True)]
    pallas_call x0 -> x1, Pallas kernels: none -> 146 us  [on_device(): pl.pallas_call(kernel, out_shape=(jax.ShapeDtypeStruct((TOK, D), BF16), j...]
    unnamed x4 -> x0, waiting for transfers between devices: 90.4 us -> none
    dot_general x11 -> x0, matrix products: 89.2 us -> none  [the longest x3 30.9 us: contract_first(): lax.dot_general(left, right, (((0,), (0,)), ((), ())), preferred_element_...]
    all_to_all x2 -> x0, blocking collectives: 40.1 us -> none  [to_owners(): lax.all_to_all(slots, 'dp', split_axis=0, concat_axis=0, tiled=True)]
    unnamed x22 -> x16, local copies, waits for them, and re-layouts: 1.56 us -> 8.21 us
    all_to_all x1 -> x0, waiting for transfers between devices: 5.59 us -> none  [to_sources(): lax.all_to_all(local_rows, 'dp', split_axis=0, concat_axis=0, tiled=True)]
    all_to_all x1 -> x0, starting transfers between devices: 5.22 us -> none  [to_sources(): lax.all_to_all(local_rows, 'dp', split_axis=0, concat_axis=0, tiled=True)]
  transfers between devices with their start and end apart: 4 -> 0, of which waited for: 4 -> 0; matrix products, arithmetic and copies ran while one was open for 10% -> 0% of each run, Pallas kernels for 0% -> 0%
where the time goes in v1:
time: 156 us; the launch traced here: 155 us
  Pallas kernels  146 us (94%)
  local copies, waits for them, and re-layouts  8.21 us (5%)
    pallas_call x1, Pallas kernels, on_device(): pl.pallas_call(kernel, out_shape=(jax.ShapeDtypeStruct((TOK, D), BF16), j...  146 us
    unnamed x16, local copies, waits for them, and re-layouts  8.21 us

profile of v1, /device:TPU:1, one launch (start us, length us, event | category | flops | bytes accessed | tf_op | source)
XLA Modules:
  0.0 155.3 jit_solution(14439513506097330996)
XLA Ops:
  0.6 0.0 copy-start.3
  0.6 0.6 copy-done.3
  1.3 0.0 copy-start.4
  1.3 0.7 copy.12.routes_ref
  2.0 0.0 copy-done.4
  2.0 0.7 copy.13.rw_ref
  2.8 146.4 %learner_step.1 = (bf16[128,4096]{1,0:T(8,128)(2,1)}, bf16[96,4096]{1,0:T(8,128)(2,1)}, bf16[96,4096]{1,0:T(8,128)(2,1)}, bf16[96,4096]{1,0:T(8,128)(2,1)}) custom-call(bf16[128,4096]{1,0:T(8,128)(2,1)} %tok_hbm.1, bf16[128,4096]{1,0:T(8,128)(2,1)} %cot_hbm.1, f32[1,4096]{1,0:T(1,128)} %bitcast.13, s32[128,1]{1,0:T(8,128)} %copy.12.routes_ref, ...), custom_call_target="tpu_custom_call" | custom-call | flops 12999999488 | bytes 9437184 | tf_op jit(solution)/shard_map/learner_step/pallas_call | solution.py:375
  149.2 0.0 copy-start.2
  149.2 2.4 %copy.18 = bf16[128,4096]{1,0:T(8,128)(2,1)} copy(bf16[128,4096]{1,0:T(8,128)(2,1)} %get-tuple-element.16) | data formatting | bytes 2097152
  151.5 0.0 copy-done.2
  151.5 0.0 copy-start.1
  151.5 0.9 copy.19
  152.4 0.5 copy-done.1
  153.0 0.0 copy-start
  153.0 0.9 copy.20
  153.8 0.5 copy-done
  154.4 0.9 copy.21
Async XLA Ops:
  0.6 0.7 copy-start.3
  1.3 0.7 copy-start.4
  149.2 2.4 %copy-start.2 = (bf16[96,4096]{1,0:T(8,128)(2,1)S(1)}, bf16[96,4096]{1,0:T(8,128)(2,1)}, u32[]{:S(2)}) copy-start(bf16[96,4096]{1,0:T(8,128)(2,1)} %get-tuple-element.9) | copy-start | bytes 2359300
  151.5 1.4 copy-start.1
  153.0 1.4 copy-start

commit v2 on v1

--- a/solution.py
+++ b/solution.py
@@ -28,11 +28,11 @@
 
 
 def kernel(
-    tok_hbm, cot_hbm, gain_ref, routes_ref, rw_ref, gate_hbm, up_hbm, down_hbm,
-    gt_hbm, gg_hbm, gu_hbm, gd_hbm,
-    tok, cot, norm, rgrad, send_n, send_g, place, inv,
+    tok_hbm, cot_hbm, gain_hbm, routes_hbm, rw_hbm, gate_hbm, up_hbm, down_hbm,
+    gt_out, gg_out, gu_out, gd_out,
+    gain_ref, routes_ref, rw_ref, tok, cot, norm, rgrad, send_n, send_g, place, place_t, weight, inv,
     rn, rg, wgu, wd, pre, hg, act, act_t, hid,
-    part, ptl, ptr, pfl, pfr, ret_send, ret, qbuf, out_t,
+    part, ptl, ptr, pfl, pfr, ret_send, ret, qbuf,
     pg, pd, gtl, gtr, gfl, gfr,
     ssem, rsem, lsem,
 ):
@@ -67,14 +67,14 @@
         sent.append(copy)
         return copy
 
-    tok_in = local(tok_hbm, tok)
-    cot_in = local(cot_hbm, cot)
-
     barrier = pltpu.get_barrier_semaphore()
     partners = [r_right, r_left, w_right, w_left]
     partners += [(lax.rem(dp + k, 8), ex) for k in range(1, 8)]
     for device in partners:
         pl.semaphore_signal(barrier, inc=1, device_id=device, device_id_type=MESH)
+    small_in = [local(routes_hbm, routes_ref), local(rw_hbm, rw_ref), local(gain_hbm, gain_ref)]
+    tok_in = local(tok_hbm, tok)
+    cot_in = local(cot_hbm, cot)
     pl.semaphore_wait(barrier, len(partners))
 
     w_from_left, w_from_right = [], []
@@ -84,15 +84,20 @@
         w_from_right.append(remote(src, buf.at[pl.ds(2 * step + at, HID)], w_left))
     w_own = [local(src, buf.at[pl.ds(at, HID)]) for src, buf, step, at in places]
 
+    for copy in small_in:
+        copy.wait()
     chosen = routes_ref[...]
     lane = lax.broadcasted_iota(jnp.int32, (TOK, TOK), 1)
     sub = lax.broadcasted_iota(jnp.int32, (TOK, TOK), 0)
-    onehot = (chosen == lane).astype(F32)
-    earlier = dot((lane < sub).astype(F32).astype(BF16), onehot.astype(BF16), 1, 0)
-    position = jnp.sum(earlier * onehot, axis=1, keepdims=True)
+    onehot = (chosen == sub).astype(F32)
+    earlier = dot(onehot.astype(BF16), (sub < lane).astype(F32).astype(BF16), 1, 0)
+    position = jnp.sum(earlier * onehot, axis=0, keepdims=True)
     piece = jnp.bitwise_and(dp - chosen + 8, 7)
     slot = piece.astype(F32) * CAP + position
-    place[...] = (slot == lane.astype(F32)).astype(F32).astype(BF16)
+    placing = (slot == sub.astype(F32)).astype(F32)
+    place[...] = placing.T.astype(BF16)
+    place_t[...] = placing.astype(BF16)
+    weight[...] = jnp.broadcast_to(rw_ref[...], (TOK, TOK)).T
 
     tok_in.wait()
     cot_in.wait()
@@ -103,12 +108,12 @@
         scale = lax.rsqrt(jnp.mean(x * x, axis=-1, keepdims=True) + 1e-06)
         inv[rows, :] = jnp.broadcast_to(scale, (16, 128))
         norm[rows, :] = ((x * scale) * gain_ref[...]).astype(BF16)
-        rgrad[rows, :] = (rw_ref[rows, :] * cot[rows, :].astype(F32)).astype(BF16)
+        rgrad[rows, :] = (weight[rows, 0:1] * cot[rows, :].astype(F32)).astype(BF16)
         return carry
 
     lax.fori_loop(0, TOK // 16, norm_rows, 0)
 
-    placing_t = place[...].astype(F32).T.astype(BF16)
+    placing_t = place_t[...]
 
     def place_rows(i, carry):
         cols = pl.ds(pl.multiple_of(i * COLS, COLS), COLS)
@@ -130,73 +135,73 @@
         arrive[k // 4].append(remote(send_n.at[piece_rows], rn.at[at_piece(k)], owner))
         arrive[k // 4].append(remote(send_g.at[piece_rows], rg.at[at_piece(k)], owner))
 
+    def row_slot(half, s, at=0, size=HALF):
+        return pl.ds(half * 256 + s * HALF + at, size)
+
+    def send_own(buf, half):
+        return (
+            remote(buf.at[row_slot(half, 0)], buf.at[row_slot(half, 1)], r_right),
+            remote(buf.at[row_slot(half, 0)], buf.at[row_slot(half, 2)], r_left),
+        )
+
+    def pass_on(buf, half, first):
+        first[0].wait_recv()
+        a = remote(buf.at[row_slot(half, 1, 0, 32)], buf.at[row_slot(half, 3, 0, 32)], r_right)
+        first[1].wait_recv()
+        b = remote(buf.at[row_slot(half, 2, 32, 32)], buf.at[row_slot(half, 3, 32, 32)], r_left)
+        return a, b
+
     w_from_left[0].wait_recv()
     w_last = [remote(wgu.at[pl.ds(192, HID)], wgu.at[pl.ds(3 * 192, HID)], w_right)]
     w_from_right[0].wait_recv()
     w_from_left[1].wait_recv()
     w_from_right[1].wait_recv()
     w_last.append(remote(wgu.at[pl.ds(2 * 192 + 96, HID)], wgu.at[pl.ds(3 * 192 + 96, HID)], w_left))
+    for copy in arrive[0]:
+        copy.wait_recv()
+    own_an = send_own(rn, 0)
+    own_ag = send_own(rg, 0)
     w_from_left[2].wait_recv()
     w_last.append(remote(wd.at[pl.ds(HID, 48)], wd.at[pl.ds(3 * HID, 48)], w_right))
     w_from_right[2].wait_recv()
     w_last.append(remote(wd.at[pl.ds(2 * HID + 48, 48)], wd.at[pl.ds(3 * HID + 48, 48)], w_left))
-
-    def row_slot(half, s, at=0, size=HALF):
-        return pl.ds(half * 256 + s * HALF + at, size)
-
-    def send_own(buf, half):
-        return (
-            remote(buf.at[row_slot(half, 0)], buf.at[row_slot(half, 1)], r_right),
-            remote(buf.at[row_slot(half, 0)], buf.at[row_slot(half, 2)], r_left),
-        )
-
-    def pass_on(buf, half, first):
-        first[0].wait_recv()
-        a = remote(buf.at[row_slot(half, 1, 0, 32)], buf.at[row_slot(half, 3, 0, 32)], r_right)
-        first[1].wait_recv()
-        b = remote(buf.at[row_slot(half, 2, 32, 32)], buf.at[row_slot(half, 3, 32, 32)], r_left)
-        return a, b
-
-    for copy in arrive[0]:
-        copy.wait_recv()
-    own_an = send_own(rn, 0)
-    own_ag = send_own(rg, 0)
     for copy in arrive[1]:
         copy.wait_recv()
     own_bn = send_own(rn, 1)
     last_a = [*pass_on(rn, 0, own_an), *pass_on(rg, 0, own_ag)]
     own_bg = send_own(rg, 1)
-    last_b = [*pass_on(rn, 1, own_bn), *pass_on(rg, 1, own_bg)]
-
-    for copy in (*w_own,):
+    last_b = [*pass_on(rn, 1, own_bn)]
+
+    for copy in w_own:
         copy.wait()
     for copy in w_last:
         copy.wait_recv()
 
+    def products(half):
+        rows = pl.ds(half * 256, 256)
+        pre[...] = dot(wgu[...], rn[rows, :], 1, 1)
+        hg[...] = dot(wd[...], rg[rows, :], 1, 1)
+
     def activations(half):
         rows = pl.ds(half * 256, 256)
 
         def per_slot(s, carry):
-            two = pl.ds(pl.multiple_of(s * 192, 96), 192)
             one = pl.ds(pl.multiple_of(s * HID, HID), HID)
-            pre[...] = dot(wgu[two, :], rn[rows, :], 1, 1)
-            hidden_grad = dot(wd[one, :], rg[rows, :], 1, 1)
-            gate = pre[pl.ds(0, HID), :]
-            up = pre[pl.ds(HID, HID), :]
+            gate_rows = pl.ds(pl.multiple_of(s * 192, 96), HID)
+            up_rows = pl.ds(pl.multiple_of(s * 192 + HID, 96), HID)
+            gate, up, hidden_grad = pre[gate_rows, :], pre[up_rows, :], hg[one, :]
             sig = jax.nn.sigmoid(gate)
             active = gate * sig
             hid[one, rows] = (active * up).astype(BF16)
-            act[pl.ds(pl.multiple_of(s * 192, 96), HID), rows] = (
-                hidden_grad * up * sig * (1.0 + gate * (1.0 - sig))
-            ).astype(BF16)
-            act[pl.ds(pl.multiple_of(s * 192 + HID, 96), HID), rows] = (hidden_grad * active).astype(BF16)
+            act[gate_rows, rows] = (hidden_grad * up * sig * (1.0 + gate * (1.0 - sig))).astype(BF16)
+            act[up_rows, rows] = (hidden_grad * active).astype(BF16)
             return carry
 
         lax.fori_loop(0, SLOTS, per_slot, 0)
 
     def partials(half):
         rows = pl.ds(half * 256, 256)
-        act_t[...] = act[:, rows].astype(F32).T.astype(BF16)
+        act_t[...] = act[:, rows].T
 
         def per_cols(i, carry):
             cols = pl.ds(pl.multiple_of(i * COLS, COLS), COLS)
@@ -271,18 +276,19 @@
 
     for copy in last_a:
         copy.wait_recv()
+    products(0)
     activations(0)
+    last_b += [*pass_on(rg, 1, own_bg)]
     partials(0)
     through_a, plain_a = scatter_start(0)
 
     for copy in last_b:
         copy.wait_recv()
+    products(1)
+    summed_a = scatter_add(0, through_a)
     activations(1)
-    summed_a = scatter_add(0, through_a)
     partials(1)
     through_b, plain_b = scatter_start(1)
-    back = scatter_end(0, [*plain_a, *summed_a])
-
     weight_grads(3)
     grad_through = [
         remote(pg.at[pl.ds(3 * 192, HID)], gtl.at[pl.ds(0, HID)], w_right),
@@ -290,6 +296,7 @@
         remote(pd.at[pl.ds(3 * HID, 48)], gtl.at[pl.ds(HID, 48)], w_right),
         remote(pd.at[pl.ds(3 * HID + 48, 48)], gtr.at[pl.ds(HID, 48)], w_left),
     ]
+    back = scatter_end(0, [*plain_a, *summed_a])
     summed_b = scatter_add(1, through_b)
     weight_grads(2)
     grad_plain = [
@@ -333,37 +340,49 @@
     def moved(i, carry):
         cols = pl.ds(pl.multiple_of(i * COLS, COLS), COLS)
         unit = tok[:, cols].astype(F32) * scale
-        out_t[:, cols] = (cot[:, cols].astype(F32) + scale * (qbuf[:, cols] - unit * mean)).astype(BF16)
+        gt_out[:, cols] = (cot[:, cols].astype(F32) + scale * (qbuf[:, cols] - unit * mean)).astype(BF16)
         return carry
 
     lax.fori_loop(0, D // COLS, moved, 0)
-    outs = [local(out_t, gt_hbm)]
-
-    def grad_end(buf, at, got, copies, dst):
+
+    def grad_end(out, buf, first, got, size, copies):
         for copy in copies:
             copy.wait_recv()
-        add_three(buf, at, got)
-        outs.append(local(buf.at[pl.ds(at, HID)], dst))
-
-    def add_three(buf, at, got):
+
         def per_rows(i, carry):
-            mine = pl.ds(pl.multiple_of(at + i * 16, 16), 16)
-            theirs = pl.ds(pl.multiple_of(got + i * 16, 16), 16)
-            buf[mine, :] = (
-                buf[mine, :].astype(F32) + gfl[theirs, :].astype(F32) + gfr[theirs, :].astype(F32)
+            mine = pl.ds(pl.multiple_of(first + i * 16, 16), 16)
+            theirs = pl.ds(pl.multiple_of(got + first + i * 16, 16), 16)
+            own = pl.ds(pl.multiple_of(got % 192 + first + i * 16, 16), 16)
+            out[mine, :] = (
+                buf[own, :].astype(F32) + gfl[theirs, :].astype(F32) + gfr[theirs, :].astype(F32)
             ).astype(BF16)
             return carry
 
-        lax.fori_loop(0, HID // 16, per_rows, 0)
-
-    grad_end(pg, 0, 0, [grad_summed[0], grad_plain[2]], gg_hbm)
-    grad_end(pg, HID, HID, [grad_plain[0], grad_summed[1]], gu_hbm)
-    grad_end(pd, 0, 2 * HID, [grad_plain[1], grad_plain[3], grad_summed[2], grad_summed[3]], gd_hbm)
-
-    for copy in outs:
+        lax.fori_loop(0, size // 16, per_rows, 0)
+
+    for copy in sent[: -len(grad_summed)]:
+        copy.wait_send()
+
+    grad_end(gg_out, pg, 0, 0, HID, [grad_summed[0], grad_plain[2]])
+    grad_end(gu_out, pg, 0, HID, HID, [grad_plain[0], grad_summed[1]])
+    grad_end(gd_out, pd, 0, 2 * HID, 48, [grad_plain[3], grad_summed[2]])
+    grad_end(gd_out, pd, 48, 2 * HID, 48, [grad_plain[1], grad_summed[3]])
+
+    for copy in grad_summed:
+        copy.wait_send()
+
+
+def hand_over(*refs):
+    copies = []
+    for i in range(4):
+        rows = refs[i].shape[0] // 2
+        for j in range(2):
+            part = pl.ds(j * rows, rows)
+            copies.append(pltpu.make_async_copy(refs[i].at[part], refs[4 + i].at[part], refs[8].at[2 * i + j]))
+    for copy in copies:
+        copy.start()
+    for copy in copies:
         copy.wait()
-    for copy in sent:
-        copy.wait_send()
 
 
 def on_device(
@@ -375,35 +394,45 @@
     outs = pl.pallas_call(
         kernel,
         out_shape=(
-            jax.ShapeDtypeStruct((TOK, D), BF16),
-            jax.ShapeDtypeStruct((HID, D), BF16),
-            jax.ShapeDtypeStruct((HID, D), BF16),
-            jax.ShapeDtypeStruct((HID, D), BF16),
+            pltpu.VMEM((TOK, D), BF16),
+            pltpu.VMEM((HID, D), BF16),
+            pltpu.VMEM((HID, D), BF16),
+            pltpu.VMEM((HID, D), BF16),
         ),
-        in_specs=[any_spec, any_spec, vmem_spec, vmem_spec, vmem_spec, any_spec, any_spec, any_spec],
-        out_specs=(any_spec,) * 4,
+        in_specs=[any_spec] * 8,
+        out_specs=(vmem_spec,) * 4,
         scratch_shapes=[
+            pltpu.VMEM((1, D), F32), pltpu.VMEM((1, TOK), jnp.int32), pltpu.VMEM((1, TOK), F32),
             rows(TOK), rows(TOK), rows(TOK), rows(TOK), rows(TOK), rows(TOK),
-            pltpu.VMEM((TOK, TOK), BF16), pltpu.VMEM((TOK, 128), F32),
+            pltpu.VMEM((TOK, TOK), BF16), pltpu.VMEM((TOK, TOK), BF16),
+            pltpu.VMEM((TOK, TOK), F32), pltpu.VMEM((TOK, 128), F32),
             rows(512), rows(512), rows(768), rows(384),
-            pltpu.VMEM((192, 256), F32), pltpu.VMEM((8, 128), F32),
+            pltpu.VMEM((768, 256), F32), pltpu.VMEM((384, 256), F32),
             pltpu.VMEM((768, 512), BF16), pltpu.VMEM((256, 768), BF16), pltpu.VMEM((384, 512), BF16),
             rows(512), rows(64), rows(64), rows(128), rows(128),
-            rows(TOK), rows(TOK), rows(TOK, F32), rows(TOK),
+            rows(TOK), rows(TOK), rows(TOK, F32),
             rows(768), rows(384), rows(144), rows(144), rows(288), rows(288),
             pltpu.SemaphoreType.DMA((N_REMOTE,)),
             pltpu.SemaphoreType.DMA((N_REMOTE,)),
             pltpu.SemaphoreType.DMA((N_LOCAL,)),
         ],
         compiler_params=pltpu.CompilerParams(
-            collective_id=0, has_side_effects=True, vmem_limit_bytes=63 * 2**20
+            collective_id=0, has_side_effects=True, vmem_limit_bytes=56 * 2**20
         ),
         cost_estimate=pl.CostEstimate(flops=13 * 10**9, bytes_accessed=9 * 2**20, transcendentals=2**18),
         name="learner_step",
     )(
-        tokens, cotangent, norm_gain.reshape(1, D), routes, route_weight,
+        tokens, cotangent, norm_gain.reshape(1, D), routes.reshape(1, TOK), route_weight.reshape(1, TOK),
         gate_weight[0], up_weight[0], down_weight[0],
     )
+    outs = pl.pallas_call(
+        hand_over,
+        out_shape=tuple(jax.ShapeDtypeStruct(out.shape, out.dtype) for out in outs),
+        in_specs=[vmem_spec] * 4,
+        out_specs=(any_spec,) * 4,
+        scratch_shapes=[pltpu.SemaphoreType.DMA((8,))],
+        name="hand_over",
+    )(*(pltpu.with_memory_space_constraint(out, pltpu.VMEM) for out in outs))
     return (outs[0], outs[1][None], outs[2][None], outs[3][None])
 
 

time: 156 us -> 141 us (0.904)
  local copies, waits for them, and re-layouts: 8.21 us -> 0 us
  Pallas kernels: 146 us -> 141 us
    unnamed x16 -> x0, local copies, waits for them, and re-layouts: 8.21 us -> none
    pallas_call x1 -> x2, Pallas kernels: 146 us -> 141 us  [the longest x1 139 us: on_device(): pl.pallas_call(kernel, out_shape=(pltpu.VMEM((TOK, D), BF16), pltpu.VMEM(...]
where the time goes in v2:
time: 141 us
  Pallas kernels  141 us (100%)
    pallas_call x1, Pallas kernels, on_device(): pl.pallas_call(kernel, out_shape=(pltpu.VMEM((TOK, D), BF16), pltpu.VMEM(...  139 us

profile of v2, /device:TPU:1, one launch (start us, length us, event | category | flops | bytes accessed | tf_op | source)
XLA Modules:
  0.0 141.3 jit_solution(3610179718420193608)
XLA Ops:
  0.6 138.8 %learner_step.1 = (bf16[128,4096]{1,0:T(8,128)(2,1)S(1)}, bf16[96,4096]{1,0:T(8,128)(2,1)S(1)}, bf16[96,4096]{1,0:T(8,128)(2,1)S(1)}, bf16[96,4096]{1,0:T(8,128)(2,1)S(1)}) custom-call(bf16[128,4096]{1,0:T(8,128)(2,1)} %tok_hbm.1, bf16[128,4096]{1,0:T(8,128)(2,1)} %cot_hbm.1, f32[1,4096]{1,0:T(1,128)} %bitcast.15, s32[1,128]{1,0:T(1,128)} %bitcast.16, ...), custom_call_target="tpu_custom_call" | custom-call | flops 12999999488 | bytes 9437184 | tf_op jit(solution)/shard_map/learner_step/pallas_call | solution.py:394
  139.5 1.8 %hand_over.1 = (bf16[128,4096]{1,0:T(8,128)(2,1)}, bf16[96,4096]{1,0:T(8,128)(2,1)}, bf16[96,4096]{1,0:T(8,128)(2,1)}, bf16[96,4096]{1,0:T(8,128)(2,1)}) custom-call(bf16[128,4096]{1,0:T(8,128)(2,1)S(1)} %get-tuple-element.12.refs_0_, bf16[96,4096]{1,0:T(8,128)(2,1)S(1)} %get-tuple-element.13.refs_1_, bf16[96,4096]{1,0:T(8,128)(2,1)S(1)} %get-tuple-element.14.refs_2_, ...), custom_call_target="tpu_custom_call" | custom-call | tf_op jit(solution)/shard_map/hand_over/pallas_call | solution.py:428

commit v3 on v2

v3 whole, which is shorter than its diff:
```python
import functools

import jax
import jax.numpy as jnp
from jax import lax
from jax.experimental import pallas as pl
from jax.experimental.pallas import tpu as pltpu
from jax.sharding import PartitionSpec as P

MESH = pl.DeviceIdType.MESH
F32, BF16 = jnp.float32, jnp.bfloat16
D = 4096
TOK = 128
CAP = 16
HID = 96
HALF = 64
COLS = 512
SLOTS = 4

N_SEND, N_RECV, N_LOCAL = 8, 34, 8


def dot(left, right, left_dim, right_dim):
    return lax.dot_general(
        left, right, (((left_dim,), (right_dim,)), ((), ())), preferred_element_type=F32
    )


def kernel(
    tok_hbm, cot_hbm, gain_hbm, routes_hbm, rw_hbm, gate_hbm, up_hbm, down_hbm,
    gt_out, gg_out, gu_out, gd_out,
    gain_ref, routes_ref, rw_ref, tok, cot, norm, rgrad, send, place, place_t, weight, inv,
    x, w, pre, hg, act, act_t, hid,
    part, ptl, ptr, pfl, pfr, ret_send, ret, qbuf,
    g, gtl, gtr, gfl, gfr,
    ssem, rsem, lsem,
):
    dp = lax.axis_index("dp")
    ex = lax.axis_index("expert")
    core = lax.rem(dp, 2)
    rstride = 1 + 3 * core
    wstride = 4 - 3 * core
    rpos = lax.rem(lax.div(ex, rstride), 4)
    wpos = lax.rem(lax.div(ex, wstride), 4)
    r_right = (dp, ex + rstride * (lax.rem(rpos + 1, 4) - rpos))
    r_left = (dp, ex + rstride * (lax.rem(rpos + 3, 4) - rpos))
    w_right = (dp, ex + wstride * (lax.rem(wpos + 1, 4) - wpos))
    w_left = (dp, ex + wstride * (lax.rem(wpos + 3, 4) - wpos))

    count = [0, 0]

    def local(src, dst):
        copy = pltpu.make_async_copy(src, dst, lsem.at[count[1]])
        count[1] += 1
        copy.start()
        return copy

    def new():
        count[0] += 1
        return count[0] - 1

    def describe(src, dst, device, sender, receiver):
        return pltpu.make_async_remote_copy(
            src_ref=src, dst_ref=dst, send_sem=ssem.at[sender], recv_sem=rsem.at[receiver],
            device_id=device, device_id_type=MESH,
        )

    def remote(src, dst, device, sender, receiver=None):
        copy = describe(src, dst, device, sender, new() if receiver is None else receiver)
        copy.start()
        return copy

    def arrived(ref, receiver):
        describe(ref, ref, r_right, 0, receiver).wait_recv()

    def left_here(ref, sender):
        describe(ref, ref, r_right, sender, 0).wait_send()

    barrier = pltpu.get_barrier_semaphore()
    partners = [r_right, r_left, w_right, w_left]
    partners += [(lax.rem(dp + k, 8), ex) for k in range(1, 8)]
    for device in partners:
        pl.semaphore_signal(barrier, inc=1, device_id=device, device_id_type=MESH)
    small_in = [local(routes_hbm, routes_ref), local(rw_hbm, rw_ref), local(gain_hbm, gain_ref)]
    tok_in = local(tok_hbm, tok)
    cot_in = local(cot_hbm, cot)
    pl.semaphore_wait(barrier, len(partners))

    gate_r = remote(gate_hbm, w.at[1, pl.ds(0, HID)], w_right, 0)
    down_l = remote(down_hbm, w.at[2, pl.ds(2 * HID, HID)], w_left, 0)
    up_r = remote(up_hbm, w.at[1, pl.ds(HID, HID)], w_right, 0)
    up_l = remote(up_hbm, w.at[2, pl.ds(HID, HID)], w_left, 0)
    down_r = remote(down_hbm, w.at[1, pl.ds(2 * HID, HID)], w_right, 0)
    gate_l = remote(gate_hbm, w.at[2, pl.ds(0, HID)], w_left, 0)
    w_own = [local(src, w.at[0, pl.ds(i * HID, HID)]) for i, src in enumerate((gate_hbm, up_hbm, down_hbm))]

    for copy in small_in:
        copy.wait()
    chosen = routes_ref[...]
    lane = lax.broadcasted_iota(jnp.int32, (TOK, TOK), 1)
    sub = lax.broadcasted_iota(jnp.int32, (TOK, TOK), 0)
    onehot = (chosen == sub).astype(F32)
    earlier = dot(onehot.astype(BF16), (sub < lane).astype(F32).astype(BF16), 1, 0)
    position = jnp.sum(earlier * onehot, axis=0, keepdims=True)
    piece = jnp.bitwise_and(dp - chosen + 8, 7)
    slot = piece.astype(F32) * CAP + position
    placing = (slot == sub.astype(F32)).astype(F32)
    place[...] = placing.T.astype(BF16)
    place_t[...] = placing.astype(BF16)
    weight[...] = jnp.broadcast_to(rw_ref[...], (TOK, TOK)).T

    tok_in.wait()
    cot_in.wait()

    def norm_rows(i, carry):
        rows = pl.ds(pl.multiple_of(i * 16, 16), 16)
        x = tok[rows, :].astype(F32)
        scale = lax.rsqrt(jnp.mean(x * x, axis=-1, keepdims=True) + 1e-06)
        inv[rows, :] = jnp.broadcast_to(scale, (16, 128))
        norm[rows, :] = ((x * scale) * gain_ref[...]).astype(BF16)
        rgrad[rows, :] = (weight[rows, 0:1] * cot[rows, :].astype(F32)).astype(BF16)
        return carry

    lax.fori_loop(0, TOK // 16, norm_rows, 0)

    placing_t = place_t[...]

    def place_rows(i, carry):
        cols = pl.ds(pl.multiple_of(i * COLS, COLS), COLS)
        send[:, 0, :, cols] = dot(placing_t, norm[:, cols], 1, 0).astype(BF16).reshape(8, CAP, COLS)
        send[:, 1, :, cols] = dot(placing_t, rgrad[:, cols], 1, 0).astype(BF16).reshape(8, CAP, COLS)
        return carry

    lax.fori_loop(0, D // COLS, place_rows, 0)

    x[0, 0, :, pl.ds(0, CAP), :] = send[0]
    pieces = [new(), new()]
    for k in range(1, 8):
        owner = (lax.rem(dp + 8 - k, 8), ex)
        remote(send.at[k], x.at[k // 4, 0, :, pl.ds((k % 4) * CAP, CAP)], owner, 1, pieces[k // 4])

    w_far = new()
    gate_r.wait_recv()
    down_l.wait_recv()
    up_r.wait_recv()
    remote(w.at[1, pl.ds(0, 144)], w.at[3, pl.ds(0, 144)], w_right, 2, w_far)
    up_l.wait_recv()
    remote(w.at[2, pl.ds(144, 144)], w.at[3, pl.ds(144, 144)], w_left, 2, w_far)

    arrived(x.at[0, 0, :, pl.ds(CAP, 3 * CAP)], pieces[0])
    a_r = remote(x.at[0, 0], x.at[0, 1], r_right, 3)
    a_l = remote(x.at[0, 0], x.at[0, 2], r_left, 3)
    arrived(x.at[1, 0], pieces[1])
    bn_r = remote(x.at[1, 0, 0], x.at[1, 1, 0], r_right, 3)
    bg_l = remote(x.at[1, 0, 1], x.at[1, 2, 1], r_left, 3)
    a_far, b_far = new(), new()
    a_r.wait_recv()
    remote(x.at[0, 1, 0], x.at[0, 3, 0], r_right, 4, a_far)
    bg_r = remote(x.at[1, 0, 1], x.at[1, 1, 1], r_right, 3)
    a_l.wait_recv()
    remote(x.at[0, 2, 1], x.at[0, 3, 1], r_left, 4, a_far)
    bn_l = remote(x.at[1, 0, 0], x.at[1, 2, 0], r_left, 3)
    bn_r.wait_recv()
    remote(x.at[1, 1, 0], x.at[1, 3, 0], r_right, 4, b_far)
    bg_l.wait_recv()
    remote(x.at[1, 2, 1], x.at[1, 3, 1], r_left, 4, b_far)

    def row_slot(half, s, at=0, size=HALF):
        return pl.ds(half * 256 + s * HALF + at, size)

    def products(half):
        pre[...] = dot(w[:, pl.ds(0, 192), :].reshape(768, D), x[half, :, 0].reshape(256, D), 1, 1)
        hg[...] = dot(w[:, pl.ds(192, HID), :].reshape(384, D), x[half, :, 1].reshape(256, D), 1, 1)

    def activations(half):
        rows = pl.ds(half * 256, 256)

        def per_slot(s, carry):
            one = pl.ds(pl.multiple_of(s * HID, HID), HID)
            gate_rows = pl.ds(pl.multiple_of(s * 192, 96), HID)
            up_rows = pl.ds(pl.multiple_of(s * 192 + HID, 96), HID)
            gate, up, hidden_grad = pre[gate_rows, :], pre[up_rows, :], hg[one, :]
            sig = jax.nn.sigmoid(gate)
            active = gate * sig
            hid[one, rows] = (active * up).astype(BF16)
            act[gate_rows, rows] = (hidden_grad * up * sig * (1.0 + gate * (1.0 - sig))).astype(BF16)
            act[up_rows, rows] = (hidden_grad * active).astype(BF16)
            return carry

        lax.fori_loop(0, SLOTS, per_slot, 0)

    def partials(half):
        rows = pl.ds(half * 256, 256)
        act_t[...] = act[:, rows].T

        def per_cols(i, carry):
            cols = pl.ds(pl.multiple_of(i * COLS, COLS), COLS)
            part[rows, cols] = dot(act_t[...], w[:, pl.ds(0, 192), cols].reshape(768, COLS), 1, 0).astype(BF16)
            return carry

        lax.fori_loop(0, D // COLS, per_cols, 0)

    def add_into(buf, start, other, at, size):
        def per_rows(i, carry):
            mine = pl.ds(pl.multiple_of(start + i * 16, 16), 16)
            theirs = pl.ds(pl.multiple_of(at + i * 16, 16), 16)
            buf[mine, :] = (buf[mine, :].astype(F32) + other[theirs, :].astype(F32)).astype(BF16)
            return carry

        lax.fori_loop(0, size // 16, per_rows, 0)

    def scatter_start(half):
        ends = [new(), new()]
        through = [
            remote(part.at[row_slot(half, 3, 0, 32)], ptl.at[pl.ds(half * 32, 32)], r_right, 5),
            remote(part.at[row_slot(half, 3, 32, 32)], ptr.at[pl.ds(half * 32, 32)], r_left, 5),
        ]
        remote(part.at[row_slot(half, 2, 32, 32)], pfl.at[pl.ds(half * 64 + 32, 32)], r_right, 5, ends[0])
        remote(part.at[row_slot(half, 1, 0, 32)], pfr.at[pl.ds(half * 64, 32)], r_left, 5, ends[1])
        return through, ends

    def scatter_add(half, through, ends):
        through[0].wait_recv()
        add_into(part, half * 256 + 2 * HALF, ptl, half * 32, 32)
        remote(part.at[row_slot(half, 2, 0, 32)], pfl.at[pl.ds(half * 64, 32)], r_right, 5, ends[0])
        through[1].wait_recv()
        add_into(part, half * 256 + HALF + 32, ptr, half * 32, 32)
        remote(part.at[row_slot(half, 1, 32, 32)], pfr.at[pl.ds(half * 64 + 32, 32)], r_left, 5, ends[1])

    back = new()

    def scatter_end(half, ends):
        arrived(pfl.at[pl.ds(half * 64, 64)], ends[0])
        arrived(pfr.at[pl.ds(half * 64, 64)], ends[1])

        def per_rows(i, carry):
            mine = pl.ds(pl.multiple_of(half * 256 + i * 16, 16), 16)
            got = pl.ds(pl.multiple_of(half * 64 + i * 16, 16), 16)
            ret_send[got, :] = (
                part[mine, :].astype(F32) + pfl[got, :].astype(F32) + pfr[got, :].astype(F32)
            ).astype(BF16)
            return carry

        lax.fori_loop(0, HALF // 16, per_rows, 0)
        for k in range(half * 4, half * 4 + 4):
            piece_rows = pl.ds(k * CAP, CAP)
            if k == 0:
                ret[piece_rows, :] = ret_send[piece_rows, :]
            else:
                remote(ret_send.at[piece_rows], ret.at[piece_rows], (lax.rem(dp + k, 8), ex), 6, back)

    def weight_grads(s):
        two = pl.ds(s * 192, 192)
        one = pl.ds(s * HID, HID)

        def per_cols(i, carry):
            cols = pl.ds(pl.multiple_of(i * COLS, COLS), COLS)
            g[s, pl.ds(0, 192), cols] = dot(act[two, :], x[:, :, 0, :, cols].reshape(512, COLS), 1, 0).astype(BF16)
            g[s, pl.ds(192, HID), cols] = dot(hid[one, :], x[:, :, 1, :, cols].reshape(512, COLS), 1, 0).astype(BF16)
            return carry

        lax.fori_loop(0, D // COLS, per_cols, 0)

    for copy in (*w_own,):
        copy.wait()
    down_r.wait_recv()
    gate_l.wait_recv()
    arrived(w.at[3], w_far)
    arrived(x.at[0, 3], a_far)
    products(0)
    activations(0)
    partials(0)
    through_a, ends_a = scatter_start(0)

    bg_r.wait_recv()
    bn_l.wait_recv()
    arrived(x.at[1, 3], b_far)
    products(1)
    scatter_add(0, through_a, ends_a)
    activations(1)
    partials(1)
    through_b, ends_b = scatter_start(1)
    weight_grads(3)
    top, low = pl.ds(0, 144), pl.ds(144, 144)
    grad_r = remote(g.at[3, top], gtl, w_right, 7)
    grad_l = remote(g.at[3, low], gtr, w_left, 7)
    scatter_end(0, ends_a)
    scatter_add(1, through_b, ends_b)
    weight_grads(2)
    plain_r = remote(g.at[2, low], gfl.at[low], w_right, 7)
    weight_grads(1)
    plain_l = remote(g.at[1, top], gfr.at[top], w_left, 7)
    scatter_end(1, ends_b)
    weight_grads(0)

    summed = []
    grad_r.wait_recv()
    for at, size in ((0, HID), (HID, 48)):
        add_into(g.at[2], at, gtl, at, size)
        rows = pl.ds(at, size)
        summed.append(remote(g.at[2, rows], gfl.at[rows], w_right, 7))
    grad_l.wait_recv()
    for at, size in ((0, HID), (HID, 48)):
        add_into(g.at[1], 144 + at, gtr, at, size)
        rows = pl.ds(144 + at, size)
        summed.append(remote(g.at[1, rows], gfr.at[rows], w_left, 7))

    arrived(ret.at[pl.ds(CAP, 7 * CAP)], back)
    scale = inv[:, 0:1]

    def scaled(i, total):
        cols = pl.ds(pl.multiple_of(i * COLS, COLS), COLS)
        q = dot(place[...], ret[:, cols], 1, 0) * gain_ref[:, cols]
        qbuf[:, cols] = q
        return total + jnp.sum(q * (tok[:, cols].astype(F32) * scale), axis=-1, keepdims=True)

    total = lax.fori_loop(0, D // COLS, scaled, jnp.zeros((TOK, 1), F32))
    mean = total * (1.0 / D)

    def moved(i, carry):
        cols = pl.ds(pl.multiple_of(i * COLS, COLS), COLS)
        unit = tok[:, cols].astype(F32) * scale
        gt_out[:, cols] = (cot[:, cols].astype(F32) + scale * (qbuf[:, cols] - unit * mean)).astype(BF16)
        return carry

    lax.fori_loop(0, D // COLS, moved, 0)

    def grad_end(out, start, first, size):
        def per_rows(i, carry):
            mine = pl.ds(pl.multiple_of(start + i * 16, 16), 16)
            at = pl.ds(pl.multiple_of(first + i * 16, 16), 16)
            out[mine, :] = (
                g[0, at, :].astype(F32) + gfl[at, :].astype(F32) + gfr[at, :].astype(F32)
            ).astype(BF16)
            return carry

        lax.fori_loop(0, size // 16, per_rows, 0)

    left_here(w.at[pl.ds(0, 2)], 0)
    left_here(send.at[pl.ds(1, 7)], 1)
    left_here(w.at[0], 2)
    left_here(x.at[0], 3)
    left_here(x.at[0, pl.ds(0, 2)], 4)
    left_here(part.at[pl.ds(0, 384)], 5)
    left_here(ret.at[pl.ds(CAP, 7 * CAP)], 6)
    plain_l.wait_recv()
    plain_r.wait_recv()
    summed[0].wait_recv()
    grad_end(gg_out, 0, 0, HID)
    summed[2].wait_recv()
    grad_end(gu_out, 48, 144, 48)
    grad_end(gd_out, 0, 192, 48)
    summed[1].wait_recv()
    grad_end(gu_out, 0, 96, 48)
    summed[3].wait_recv()
    grad_end(gd_out, 48, 240, 48)
    left_here(g.at[pl.ds(0, 3)], 7)


def hand_over(*refs):
    copies = []
    for i in range(4):
        rows = refs[i].shape[0] // 2
        for j in range(2):
            part = pl.ds(j * rows, rows)
            copies.append(pltpu.make_async_copy(refs[i].at[part], refs[4 + i].at[part], refs[8].at[2 * i + j]))
    for copy in copies:
        copy.start()
    for copy in copies:
        copy.wait()


def on_device(
    tokens, norm_gain, routes, route_weight, gate_weight, up_weight, down_weight, cotangent
):
    any_spec = pl.BlockSpec(memory_space=pl.ANY)
    vmem_spec = pl.BlockSpec(memory_space=pltpu.VMEM)
    rows = lambda n, t=BF16: pltpu.VMEM((n, D), t)
    outs = pl.pallas_call(
        kernel,
        out_shape=(
            pltpu.VMEM((TOK, D), BF16),
            pltpu.VMEM((HID, D), BF16),
            pltpu.VMEM((HID, D), BF16),
            pltpu.VMEM((HID, D), BF16),
        ),
        in_specs=[any_spec] * 8,
        out_specs=(vmem_spec,) * 4,
        scratch_shapes=[
            pltpu.VMEM((1, D), F32), pltpu.VMEM((1, TOK), jnp.int32), pltpu.VMEM((1, TOK), F32),
            rows(TOK), rows(TOK), rows(TOK), rows(TOK),
            pltpu.VMEM((8, 2, CAP, D), BF16),
            pltpu.VMEM((TOK, TOK), BF16), pltpu.VMEM((TOK, TOK), BF16),
            pltpu.VMEM((TOK, TOK), F32), pltpu.VMEM((TOK, 128), F32),
            pltpu.VMEM((2, SLOTS, 2, HALF, D), BF16), pltpu.VMEM((SLOTS, 3 * HID, D), BF16),
            pltpu.VMEM((768, 256), F32), pltpu.VMEM((384, 256), F32),
            pltpu.VMEM((768, 512), BF16), pltpu.VMEM((256, 768), BF16), pltpu.VMEM((384, 512), BF16),
            rows(512), rows(64), rows(64), rows(128), rows(128),
            rows(TOK), rows(TOK), rows(TOK, F32),
            pltpu.VMEM((SLOTS, 3 * HID, D), BF16), rows(144), rows(144), rows(288), rows(288),
            pltpu.SemaphoreType.DMA((N_SEND,)),
            pltpu.SemaphoreType.DMA((N_RECV,)),
            pltpu.SemaphoreType.DMA((N_LOCAL,)),
        ],
        compiler_params=pltpu.CompilerParams(
            collective_id=0, has_side_effects=True, vmem_limit_bytes=56 * 2**20
        ),
        cost_estimate=pl.CostEstimate(flops=13 * 10**9, bytes_accessed=9 * 2**20, transcendentals=2**18),
        name="learner_step",
    )(
        tokens, cotangent, norm_gain.reshape(1, D), routes.reshape(1, TOK), route_weight.reshape(1, TOK),
        gate_weight[0], up_weight[0], down_weight[0],
    )
    outs = pl.pallas_call(
        hand_over,
        out_shape=tuple(jax.ShapeDtypeStruct(out.shape, out.dtype) for out in outs),
        in_specs=[vmem_spec] * 4,
        out_specs=(any_spec,) * 4,
        scratch_shapes=[pltpu.SemaphoreType.DMA((8,))],
        name="hand_over",
    )(*(pltpu.with_memory_space_constraint(out, pltpu.VMEM) for out in outs))
    return (outs[0], outs[1][None], outs[2][None], outs[3][None])


def solution(mesh):
    token_spec = P(("dp", "expert"), None)
    weight_spec = P("dp", "expert", None)
    return jax.shard_map(
        on_device,
        mesh=mesh,
        in_specs=(token_spec, P(), token_spec, token_spec, weight_spec, weight_spec, weight_spec, token_spec),
        out_specs=(token_spec, weight_spec, weight_spec, weight_spec),
        check_vma=False,
    )
```

time: 141 us -> 139 us (0.986)
  Pallas kernels: 141 us -> 138 us
    pallas_call x1, Pallas kernels: 139 us -> 136 us  [on_device(): pl.pallas_call(kernel, out_shape=(pltpu.VMEM((TOK, D), BF16), pltpu.VMEM(...]
where the time goes in v3:
time: 139 us
  Pallas kernels  138 us (99%)
    pallas_call x1, Pallas kernels, on_device(): pl.pallas_call(kernel, out_shape=(pltpu.VMEM((TOK, D), BF16), pltpu.VMEM(...  136 us

profile of v3, /device:TPU:1, one launch (start us, length us, event | category | flops | bytes accessed | tf_op | source)
XLA Modules:
  0.0 138.7 jit_solution(14766847782204476500)
XLA Ops:
  0.6 136.2 %learner_step.1 = (bf16[128,4096]{1,0:T(8,128)(2,1)S(1)}, bf16[96,4096]{1,0:T(8,128)(2,1)S(1)}, bf16[96,4096]{1,0:T(8,128)(2,1)S(1)}, bf16[96,4096]{1,0:T(8,128)(2,1)S(1)}) custom-call(bf16[128,4096]{1,0:T(8,128)(2,1)} %tok_hbm.1, bf16[128,4096]{1,0:T(8,128)(2,1)} %cot_hbm.1, f32[1,4096]{1,0:T(1,128)} %bitcast.15, s32[1,128]{1,0:T(1,128)} %bitcast.16, ...), custom_call_target="tpu_custom_call" | custom-call | flops 12999999488 | bytes 9437184 | tf_op jit(solution)/shard_map/learner_step/pallas_call | solution.py:379
  136.9 1.8 %hand_over.1 = (bf16[128,4096]{1,0:T(8,128)(2,1)}, bf16[96,4096]{1,0:T(8,128)(2,1)}, bf16[96,4096]{1,0:T(8,128)(2,1)}, bf16[96,4096]{1,0:T(8,128)(2,1)}) custom-call(bf16[128,4096]{1,0:T(8,128)(2,1)S(1)} %get-tuple-element.12.refs_0_, bf16[96,4096]{1,0:T(8,128)(2,1)S(1)} %get-tuple-element.13.refs_1_, bf16[96,4096]{1,0:T(8,128)(2,1)S(1)} %get-tuple-element.14.refs_2_, ...), custom_call_target="tpu_custom_call" | custom-call | tf_op jit(solution)/shard_map/hand_over/pallas_call | solution.py:414
